TPU v7x, 1024 devices: a whole 4x4x32 slice. The times are simulated.
1024 devices in a mesh: rep: 32 (over x, y, core), fsdp: 32 (over z).
Axes of the slice: x: 4, y: 4, z: 32, core: 2. Of those that a mesh axis runs over, the one named last changes fastest.
Arguments:
- partials: bfloat16 [32, 64, 512, 512], P('rep', None, 'fsdp'), may hold values from -2.6 to 2.6
- owner: int32 [64], P('rep'), may hold values from 0 to 31, as said below
- left_stats: bfloat16 [64, 512, 512], P('rep', 'fsdp'), may hold values from -1.2 to 9.2, as said below
- right_stats: bfloat16 [64, 512, 512], P('rep', 'fsdp'), may hold values from -1.2 to 9.2, as said below
- left_root: bfloat16 [64, 512, 512], P('rep', 'fsdp'), may hold values from -0.6 to 4.6, as said below
- right_root: bfloat16 [64, 512, 512], P('rep', 'fsdp'), may hold values from -0.6 to 4.6, as said below
Outputs:
- update: bfloat16 [64, 512, 512], P('rep', 'fsdp')
- new_left: bfloat16 [64, 512, 512], P('rep', 'fsdp')
- new_right: bfloat16 [64, 512, 512], P('rep', 'fsdp')
Inputs may be any that keep to these rules, and one draw needn't show every extreme that they name: Within each group of 2 blocks (block b is in group b // 2) at most 2 blocks share an owner, and in some group of every draw 2 do. `left_stats`: symmetric blocks. `right_stats`: symmetric blocks. `left_root`: symmetric blocks. `right_root`: symmetric blocks.
All inputs are finite; a program needn't handle non-finite values.
Results may differ from a plain program's by a relative error of at most 0.023.
Values may be sent and summed in bfloat16 or wider, within the bound.
No kernel may reach another device: no remote copies, remote signals or barrier semaphores. Data moves between devices by JAX's collectives and lax.ppermute only.
A program may use at most 32 MiB of HBM per device.

v0:
```python
import jax
import jax.numpy as jnp
from jax import lax
from jax.experimental import pallas as pl
from jax.experimental.pallas import tpu as pltpu
from jax.sharding import Mesh, PartitionSpec as P

BETA = 0.9
EPS = 1e-06
NARROW = jnp.bfloat16
WIDE = jnp.float32
REP = ("x", "y", "c")
EVERY = ("x", "y", "c", "z")


def turned(xy, half):
    return {0: half // 2, half // 2: 0}.get(xy, xy)


def index_of(device, half):
    return turned(device // 2, half) + half * (1 - device % 2)


def routes(n_rep, n_z):
    half = n_rep // 2
    across, along, home, planes = [], [], [], [[] for _ in range(n_z)]
    for g in range(n_rep):
        for z in range(n_z):
            plane = g // 2 + half * (1 - g % 2)
            q = (plane + z) % n_rep
            via = (turned(q % half, half) * 2 + 1 - q // half) * n_z
            across.append((g * n_z + z, via + z))
            along.append((via + z, via + plane))
            home.append((via + plane, g * n_z + z))
            planes[z].append(via + z)
    return across, along, home, planes


def mm(a, b, left, right):
    return lax.dot_general(a, b, (((left,), (right,)), ((), ())), preferred_element_type=WIDE)


def half_of(roots, plane, n_z):
    order = roots.shape[-1]
    tile = order // 4
    band = plane // (n_z // 4)
    twice = jnp.concatenate([roots, roots], axis=-1)
    near = lax.select_n(band, *[twice[..., k * tile : (k + 2) * tile] for k in range(4)])
    far = lax.select_n(band, *[twice[:, k // 2, :, (k + 2) * tile : (k + 3) * tile] for k in range(4)])
    return jnp.concatenate([near[:, 0], near[:, 1], far], axis=-1)


def block_kernel(where_ref, slabs_ref, keep_ref, send_ref, grad_ref, roots_ref, second_ref):
    n_slabs, n_rows, _ = slabs_ref.shape
    order = grad_ref.shape[0]
    tile = order // 4
    half = n_slabs // 2
    plane, slabs_here = where_ref[0], (where_ref[1], where_ref[2])

    def slab_of(device):
        return (index_of(device, half) + n_slabs - plane) % n_slabs

    def first_row(slab):
        return pl.multiple_of(slab * n_rows, n_rows)

    for device in range(n_slabs):
        rows = pl.ds(first_row(slab_of(device)), n_rows)
        band = slab_of(device) // (n_slabs // 4)
        columns = [pl.ds(pl.multiple_of((band + k) % 4 * tile, tile), tile) for k in range(3)]
        grad_ref[rows, :] = slabs_ref[device, :, :order]
        for number, (side, k) in enumerate(((0, 0), (0, 1), (1, 0), (1, 1), (band // 2, 2))):
            start = order + number * tile
            roots_ref[side, rows, columns[k]] = slabs_ref[device, :, start : start + tile]
    for band in range(4):
        for side, k in ((0, 1), (1, 1), (band // 2, 2)):
            across = (band + k) % 4 * tile
            there, here = pl.ds(across, tile), pl.ds(band * tile, tile)
            roots_ref[side, there, here] = roots_ref[side, here, there].T
    grad = grad_ref[...]
    first = mm(roots_ref[0], grad, 1, 0).astype(NARROW)
    second = mm(first, roots_ref[1], 1, 0)
    second_ref[...] = second
    wide = grad.astype(WIDE)
    entries = order * order
    factor = jnp.sqrt(jnp.sum(wide * wide) / entries + EPS) / jnp.sqrt(jnp.sum(second * second) / entries + EPS)

    starts = [first_row(slab) for slab in slabs_here]
    mine = jnp.concatenate([grad_ref[pl.ds(start, n_rows), :] for start in starts], axis=0)
    row = lax.broadcasted_iota(jnp.int32, (2 * n_rows, order), 0)
    column = lax.broadcasted_iota(jnp.int32, (2 * n_rows, order), 1)
    pick = (column == jnp.where(row < n_rows, starts[0] + row, starts[1] + row - n_rows)).astype(NARROW)
    columns = mm(pick, grad, 1, 1).astype(NARROW)
    left_gram = mm(mine, grad, 1, 1).astype(NARROW)
    right_gram = mm(columns, grad, 1, 0).astype(NARROW)
    for number, out_ref in enumerate((keep_ref, send_ref)):
        out_ref[0] = (second_ref[pl.ds(starts[number], n_rows), :] * factor).astype(NARROW)
        out_ref[1] = left_gram[number * n_rows : (number + 1) * n_rows]
        out_ref[2] = right_gram[number * n_rows : (number + 1) * n_rows]


def block_rows(where, slabs, order):
    n_rows = slabs.shape[1]
    out = jax.ShapeDtypeStruct((3, n_rows, order), NARROW)
    vmem = pl.BlockSpec(memory_space=pltpu.VMEM)
    return pl.pallas_call(
        block_kernel,
        out_shape=(out, out),
        in_specs=[pl.BlockSpec(memory_space=pltpu.SMEM), vmem],
        out_specs=(vmem, vmem),
        scratch_shapes=[
            pltpu.VMEM((order, order), NARROW),
            pltpu.VMEM((2, order, order), NARROW),
            pltpu.VMEM((order, order), WIDE),
        ],
        compiler_params=pltpu.CompilerParams(vmem_limit_bytes=24 * 1024 * 1024),
        name="block_rows",
    )(where, slabs)


def local(partials, owner, left_stats, right_stats, left_root, right_root):
    n_y, n_z = lax.axis_size("y"), lax.axis_size("z")
    n_rep = lax.axis_size("x") * n_y * 2
    half = n_rep // 2
    core, plane = lax.axis_index("c"), lax.axis_index("z")
    my_xy = lax.axis_index("x") * n_y + lax.axis_index("y")
    _, _, n_rows, order = partials.shape
    across, along, home, planes = routes(n_rep, n_z)

    pieces = partials[0].reshape(n_rep, 2, n_rows, order)
    pieces = lax.all_to_all(pieces, EVERY, 0, 0, axis_index_groups=planes, tiled=True)
    grad = jnp.sum(pieces.astype(WIDE), axis=0).astype(NARROW)

    swapped = owner[1] < owner[0]
    roots = jnp.stack([left_root, right_root], axis=1)
    roots = jnp.where(swapped, roots[::-1], roots)
    roots = lax.ppermute(half_of(roots, plane, n_z), EVERY, across)
    slab = jnp.concatenate([grad, roots], axis=-1)
    slab = lax.ppermute(slab, EVERY, along)

    slabs = jnp.broadcast_to(slab[None], (half, *slab.shape)).reshape(n_rep, n_rows, slab.shape[-1])
    slabs = lax.all_to_all(slabs, REP, 0, 0, tiled=True)
    index = jnp.array([index_of(2 * xy, half) for xy in range(half)], jnp.int32)[my_xy]
    here = [(index + half * core + n_z - plane) % n_rep, (index + half * (1 - core) + n_z - plane) % n_rep]
    keep, send = block_rows(jnp.stack([plane, *here]).astype(jnp.int32), slabs, order)

    got = lax.ppermute(send, "c", [(0, 1), (1, 0)])
    both = jnp.stack([jnp.where(core == 0, keep, got), jnp.where(core == 0, got, keep)], axis=1)
    both = lax.ppermute(both, EVERY, home)
    update, left_gram, right_gram = both[0], both[1].astype(WIDE), both[2].astype(WIDE)
    scale = (1.0 - BETA) / order
    new_left = (BETA * left_stats.astype(WIDE) + scale * left_gram).astype(NARROW)
    new_right = (BETA * right_stats.astype(WIDE) + scale * right_gram).astype(NARROW)
    return update, new_left, new_right


def solution(mesh, grid=(4, 4, 2)):
    n_z = mesh.devices.shape[1]
    fine = Mesh(mesh.devices.reshape(*grid, n_z), EVERY)
    rows = P(REP, "z", None)
    return jax.shard_map(
        local,
        mesh=fine,
        in_specs=(P(REP, None, "z", None), P(REP), rows, rows, rows, rows),
        out_specs=(rows, rows, rows),
        check_vma=False,
    )
```

profile of v0, /device:TPU:8, one launch (start us, length us, event | category | flops | bytes accessed | tf_op | source)
XLA Modules:
  0.0 114.2 jit_solution(10407265201422038746)
XLA Ops:
  0.6 0.0 copy-start.4
  0.6 0.0 copy-start
  0.7 0.0 copy-start.1
  0.7 17.6 %all-to-all-start = ((bf16[32,2,16,512]{3,2,1,0:T(8,128)(2,1)}), bf16[32,2,16,512]{3,2,1,0:T(8,128)(2,1)S(1)}, u32[]{:S(2)}, u32[]{:S(2)}) async-start(bf16[32,2,16,512]{3,2,1,0:T(8,128)(2,1)} %bitcast.37), calls=%async_computation | async-start | bytes 2097152 | tf_op jit(solution)/shard_map/all_to_all | solution.py:130
  18.3 0.0 copy-done.4
  18.3 0.6 fusion.6
  20.2 0.0 copy-done
  20.2 0.0 copy-done.1
  20.4 0.7 collective-permute-start
  21.0 11.1 %all-to-all-done = bf16[32,2,16,512]{3,2,1,0:T(8,128)(2,1)S(1)} async-done(((bf16[32,2,16,512]{3,2,1,0:T(8,128)(2,1)}), bf16[32,2,16,512]{3,2,1,0:T(8,128)(2,1)S(1)}, u32[]{:S(2)}, u32[]{:S(2)}) %all-to-all-start) | async-done | bytes 1048608 | tf_op jit(solution)/shard_map/all_to_all | solution.py:130
  32.1 0.2 reduce_sum.12
  32.3 0.0 collective-permute-done
  32.3 19.6 %collective-permute-start.1 = (bf16[2,16,1152]{2,1,0:T(8,128)(2,1)S(1)}, bf16[2,16,1152]{2,1,0:T(8,128)(2,1)S(1)}, u32[]{:S(2)}, u32[]{:S(2)}) collective-permute-start(bf16[2,16,1152]{2,1,0:T(8,128)(2,1)S(1)} %pad_maximum_fusion.1), channel_id=1, source_target_pairs={{512,528},{65,80},{130,144},{195,208},{260,272},{325,336},{390,400... | collective-permute-start | bytes 221192 | tf_op jit(solution)/shard_map/ppermute | solution.py:138
  51.9 4.2 %collective-permute-done.1 = bf16[2,16,1152]{2,1,0:T(8,128)(2,1)S(1)} collective-permute-done((bf16[2,16,1152]{2,1,0:T(8,128)(2,1)S(1)}, bf16[2,16,1152]{2,1,0:T(8,128)(2,1)S(1)}, u32[]{:S(2)}, u32[]{:S(2)}) %collective-permute-start.1) | collective-permute-done | bytes 73760 | tf_op jit(solution)/shard_map/ppermute | solution.py:138
  56.1 1.1 broadcast_in_dim.2
  57.2 0.0 copy-start.5
  57.2 8.2 %all-to-all-start.1 = ((bf16[32,16,1152]{2,1,0:T(8,128)(2,1)}), bf16[32,16,1152]{2,1,0:T(8,128)(2,1)S(1)}, u32[]{:S(2)}, u32[]{:S(2)}) async-start(bf16[32,16,1152]{2,1,0:T(8,128)(2,1)} %bitcast.11), calls=%async_computation.1 | async-start | bytes 2359296 | tf_op jit(solution)/shard_map/all_to_all | solution.py:141
  65.4 0.0 copy-start.2
  65.4 0.0 copy-start.3
  65.5 0.0 copy-done.5
  65.5 0.6 dynamic_slice.3
  67.4 0.1 pad_add_fusion.where_ref
  67.5 14.8 %all-to-all-done.1.slabs_ref = bf16[32,16,1152]{2,1,0:T(8,128)(2,1)S(1)} async-done(((bf16[32,16,1152]{2,1,0:T(8,128)(2,1)}), bf16[32,16,1152]{2,1,0:T(8,128)(2,1)S(1)}, u32[]{:S(2)}, u32[]{:S(2)}) %all-to-all-start.1) | async-done | bytes 1179680 | tf_op jit(solution)/shard_map/all_to_all | solution.py:141
  82.3 2.5 %block_rows.1 = (bf16[3,16,512]{2,1,0:T(8,128)(2,1)S(1)}, bf16[3,16,512]{2,1,0:T(8,128)(2,1)S(1)}) custom-call(s32[3]{0:T(128)S(1)} %pad_add_fusion.where_ref, bf16[32,16,1152]{2,1,0:T(8,128)(2,1)S(1)} %all-to-all-done.1.slabs_ref), custom_call_target="tpu_custom_call" | custom-call | tf_op jit(solution)/shard_map/block_rows/pallas_call | solution.py:105
  84.9 1.9 %collective-permute-start.2 = (bf16[3,16,512]{2,1,0:T(8,128)(2,1)S(1)}, bf16[3,16,512]{2,1,0:T(8,128)(2,1)S(1)}, u32[]{:S(2)}, u32[]{:S(2)}) collective-permute-start(bf16[3,16,512]{2,1,0:T(8,128)(2,1)S(1)} %get-tuple-element.6), channel_id=1, source_target_pairs={{0,32},{32,0},{1,33},{33,1},{2,34},{34,2},{3,35},{35,3},{4,36},{36... | collective-permute-start | bytes 147464 | tf_op jit(solution)/shard_map/ppermute | solution.py:146
  86.8 1.2 %collective-permute-done.2 = bf16[3,16,512]{2,1,0:T(8,128)(2,1)S(1)} collective-permute-done((bf16[3,16,512]{2,1,0:T(8,128)(2,1)S(1)}, bf16[3,16,512]{2,1,0:T(8,128)(2,1)S(1)}, u32[]{:S(2)}, u32[]{:S(2)}) %collective-permute-start.2) | collective-permute-done | bytes 49184 | tf_op jit(solution)/shard_map/ppermute | solution.py:146
  88.0 17.8 %collective-permute-start.3 = (bf16[3,2,16,512]{3,2,0,1:T(8,128)(2,1)S(1)}, bf16[3,2,16,512]{3,2,0,1:T(8,128)(2,1)S(1)}, u32[]{:S(2)}, u32[]{:S(2)}) collective-permute-start(bf16[3,2,16,512]{3,2,0,1:T(8,128)(2,1)S(1)} %pad_maximum_fusion), channel_id=1, source_target_pairs={{528,0},{80,1},{144,2},{208,3},{272,4},{336,5},{400,6},{464,7},{16... | collective-permute-start | bytes 294920 | tf_op jit(solution)/shard_map/ppermute | solution.py:148
  105.8 7.1 %collective-permute-done.3 = bf16[3,2,16,512]{3,2,0,1:T(8,128)(2,1)S(1)} collective-permute-done((bf16[3,2,16,512]{3,2,0,1:T(8,128)(2,1)S(1)}, bf16[3,2,16,512]{3,2,0,1:T(8,128)(2,1)S(1)}, u32[]{:S(2)}, u32[]{:S(2)}) %collective-permute-start.3) | collective-permute-done | bytes 98336 | tf_op jit(solution)/shard_map/ppermute | solution.py:148
  112.9 0.6 slice_bitcast_fusion.1
  113.5 0.0 copy-done.2
  113.5 0.0 copy-done.3
  113.5 0.7 fusion
  (9 shorter events, 0.1 us)
Async XLA Ops:
  0.6 17.7 %copy-start.4 = (s32[2]{0:T(128)S(1)}, s32[2]{0:T(128)}, u32[]{:S(2)}) copy-start(s32[2]{0:T(128)} %param.8) | copy-start | bytes 28
  0.6 19.6 %copy-start = (bf16[2,16,512]{2,1,0:T(8,128)(2,1)S(1)}, bf16[2,16,512]{2,1,0:T(8,128)(2,1)}, u32[]{:S(2)}) copy-start(bf16[2,16,512]{2,1,0:T(8,128)(2,1)} %param.12) | copy-start | bytes 98308
  0.7 19.6 %copy-start.1 = (bf16[2,16,512]{2,1,0:T(8,128)(2,1)S(1)}, bf16[2,16,512]{2,1,0:T(8,128)(2,1)}, u32[]{:S(2)}) copy-start(bf16[2,16,512]{2,1,0:T(8,128)(2,1)} %param.11) | copy-start | bytes 98308
  0.7 31.5 %all-to-all-start = ((bf16[32,2,16,512]{3,2,1,0:T(8,128)(2,1)}), bf16[32,2,16,512]{3,2,1,0:T(8,128)(2,1)S(1)}, u32[]{:S(2)}, u32[]{:S(2)}) async-start(bf16[32,2,16,512]{3,2,1,0:T(8,128)(2,1)} %bitcast.37), calls=%async_computation | async-start | bytes 2097152 | tf_op jit(solution)/shard_map/all_to_all | solution.py:130
  20.4 11.9 %collective-permute-start = (bf16[2,16,640]{2,1,0:T(8,128)(2,1)S(1)}, bf16[2,16,640]{2,1,0:T(8,128)(2,1)S(1)}, u32[]{:S(2)}, u32[]{:S(2)}) collective-permute-start(bf16[2,16,640]{2,1,0:T(8,128)(2,1)S(1)} %pad_maximum_fusion.3), channel_id=1, source_target_pairs={{0,512},{1,65},{2,130},{3,195},{4,260},{5,325},{6,390},{7,455},{8,... | collective-permute-start | bytes 122888 | tf_op jit(solution)/shard_map/ppermute | solution.py:136
  32.3 23.8 %collective-permute-start.1 = (bf16[2,16,1152]{2,1,0:T(8,128)(2,1)S(1)}, bf16[2,16,1152]{2,1,0:T(8,128)(2,1)S(1)}, u32[]{:S(2)}, u32[]{:S(2)}) collective-permute-start(bf16[2,16,1152]{2,1,0:T(8,128)(2,1)S(1)} %pad_maximum_fusion.1), channel_id=1, source_target_pairs={{512,528},{65,80},{130,144},{195,208},{260,272},{325,336},{390,400... | collective-permute-start | bytes 221192 | tf_op jit(solution)/shard_map/ppermute | solution.py:138
  57.2 8.3 %copy-start.5 = (s32[16]{0:T(128)S(1)}, s32[16]{0:T(128)}, u32[]{:S(2)}) copy-start(s32[16]{0:T(128)} %constant.69.clone) | copy-start | bytes 196
  57.2 25.1 %all-to-all-start.1 = ((bf16[32,16,1152]{2,1,0:T(8,128)(2,1)}), bf16[32,16,1152]{2,1,0:T(8,128)(2,1)S(1)}, u32[]{:S(2)}, u32[]{:S(2)}) async-start(bf16[32,16,1152]{2,1,0:T(8,128)(2,1)} %bitcast.11), calls=%async_computation.1 | async-start | bytes 2359296 | tf_op jit(solution)/shard_map/all_to_all | solution.py:141
  65.4 48.1 %copy-start.2 = (bf16[2,16,512]{2,1,0:T(8,128)(2,1)S(1)}, bf16[2,16,512]{2,1,0:T(8,128)(2,1)}, u32[]{:S(2)}) copy-start(bf16[2,16,512]{2,1,0:T(8,128)(2,1)} %param.10) | copy-start | bytes 98308
  65.4 48.1 %copy-start.3 = (bf16[2,16,512]{2,1,0:T(8,128)(2,1)S(1)}, bf16[2,16,512]{2,1,0:T(8,128)(2,1)}, u32[]{:S(2)}) copy-start(bf16[2,16,512]{2,1,0:T(8,128)(2,1)} %param.9) | copy-start | bytes 98308
  84.9 3.1 %collective-permute-start.2 = (bf16[3,16,512]{2,1,0:T(8,128)(2,1)S(1)}, bf16[3,16,512]{2,1,0:T(8,128)(2,1)S(1)}, u32[]{:S(2)}, u32[]{:S(2)}) collective-permute-start(bf16[3,16,512]{2,1,0:T(8,128)(2,1)S(1)} %get-tuple-element.6), channel_id=1, source_target_pairs={{0,32},{32,0},{1,33},{33,1},{2,34},{34,2},{3,35},{35,3},{4,36},{36... | collective-permute-start | bytes 147464 | tf_op jit(solution)/shard_map/ppermute | solution.py:146
  88.0 24.9 %collective-permute-start.3 = (bf16[3,2,16,512]{3,2,0,1:T(8,128)(2,1)S(1)}, bf16[3,2,16,512]{3,2,0,1:T(8,128)(2,1)S(1)}, u32[]{:S(2)}, u32[]{:S(2)}) collective-permute-start(bf16[3,2,16,512]{3,2,0,1:T(8,128)(2,1)S(1)} %pad_maximum_fusion), channel_id=1, source_target_pairs={{528,0},{80,1},{144,2},{208,3},{272,4},{336,5},{400,6},{464,7},{16... | collective-permute-start | bytes 294920 | tf_op jit(solution)/shard_map/ppermute | solution.py:148
where the time goes:
time: 115 us; the launch traced here: 114 us
  starting transfers between devices  65.9 us (57%)
  waiting for transfers between devices  38.4 us (33%)
  between operations  3.51 us (3%)
  local copies, waits for them, and re-layouts  2.93 us (3%)
  Pallas kernels  2.55 us (2%)
    ppermute x1, starting transfers between devices, local(): slab = lax.ppermute(slab, EVERY, along)  19.6 us
    ppermute x1, starting transfers between devices, local(): both = lax.ppermute(both, EVERY, home)  17.8 us
    all_to_all x1, starting transfers between devices, local(): lax.all_to_all(pieces, EVERY, 0, 0, axis_index_groups=planes, tiled=True)  17.6 us
    all_to_all x1, waiting for transfers between devices, local(): slabs = lax.all_to_all(slabs, REP, 0, 0, tiled=True)  14.8 us
    all_to_all x1, waiting for transfers between devices, local(): lax.all_to_all(pieces, EVERY, 0, 0, axis_index_groups=planes, tiled=True)  11.1 us
    all_to_all x1, starting transfers between devices, local(): slabs = lax.all_to_all(slabs, REP, 0, 0, tiled=True)  8.2 us
    ppermute x1, waiting for transfers between devices, local(): both = lax.ppermute(both, EVERY, home)  7.08 us
    ppermute x1, waiting for transfers between devices, local(): slab = lax.ppermute(slab, EVERY, along)  4.16 us
  transfers between devices with their start and end apart: 6, of which 5 were waited for; matrix products, arithmetic and copies ran while one was open for 1% of the time, Pallas kernels for 0%

commit v1 on v0

--- a/solution.py
+++ b/solution.py
@@ -50,8 +50,8 @@
     return jnp.concatenate([near[:, 0], near[:, 1], far], axis=-1)
 
 
-def block_kernel(where_ref, slabs_ref, keep_ref, send_ref, grad_ref, roots_ref, second_ref):
-    n_slabs, n_rows, _ = slabs_ref.shape
+def block_kernel(where_ref, grads_ref, halves_ref, keep_ref, send_ref, grad_ref, roots_ref, second_ref):
+    n_slabs, n_rows, _ = grads_ref.shape
     order = grad_ref.shape[0]
     tile = order // 4
     half = n_slabs // 2
@@ -67,10 +67,10 @@
         rows = pl.ds(first_row(slab_of(device)), n_rows)
         band = slab_of(device) // (n_slabs // 4)
         columns = [pl.ds(pl.multiple_of((band + k) % 4 * tile, tile), tile) for k in range(3)]
-        grad_ref[rows, :] = slabs_ref[device, :, :order]
+        grad_ref[rows, :] = grads_ref[device]
         for number, (side, k) in enumerate(((0, 0), (0, 1), (1, 0), (1, 1), (band // 2, 2))):
-            start = order + number * tile
-            roots_ref[side, rows, columns[k]] = slabs_ref[device, :, start : start + tile]
+            start = number * tile
+            roots_ref[side, rows, columns[k]] = halves_ref[device, :, start : start + tile]
     for band in range(4):
         for side, k in ((0, 1), (1, 1), (band // 2, 2)):
             across = (band + k) % 4 * tile
@@ -98,14 +98,14 @@
         out_ref[2] = right_gram[number * n_rows : (number + 1) * n_rows]
 
 
-def block_rows(where, slabs, order):
-    n_rows = slabs.shape[1]
+def block_rows(where, grads, halves):
+    _, n_rows, order = grads.shape
     out = jax.ShapeDtypeStruct((3, n_rows, order), NARROW)
     vmem = pl.BlockSpec(memory_space=pltpu.VMEM)
     return pl.pallas_call(
         block_kernel,
         out_shape=(out, out),
-        in_specs=[pl.BlockSpec(memory_space=pltpu.SMEM), vmem],
+        in_specs=[pl.BlockSpec(memory_space=pltpu.SMEM), vmem, vmem],
         out_specs=(vmem, vmem),
         scratch_shapes=[
             pltpu.VMEM((order, order), NARROW),
@@ -114,7 +114,7 @@
         ],
         compiler_params=pltpu.CompilerParams(vmem_limit_bytes=24 * 1024 * 1024),
         name="block_rows",
-    )(where, slabs)
+    )(where, grads, halves)
 
 
 def local(partials, owner, left_stats, right_stats, left_root, right_root):
@@ -137,11 +137,13 @@
     slab = jnp.concatenate([grad, roots], axis=-1)
     slab = lax.ppermute(slab, EVERY, along)
 
-    slabs = jnp.broadcast_to(slab[None], (half, *slab.shape)).reshape(n_rep, n_rows, slab.shape[-1])
-    slabs = lax.all_to_all(slabs, REP, 0, 0, tiled=True)
+    slabs = []
+    for part in (slab[..., :order], slab[..., order:]):
+        copies = jnp.broadcast_to(part[None], (half, *part.shape)).reshape(n_rep, n_rows, part.shape[-1])
+        slabs.append(lax.all_to_all(copies, REP, 0, 0, tiled=True))
     index = jnp.array([index_of(2 * xy, half) for xy in range(half)], jnp.int32)[my_xy]
     here = [(index + half * core + n_z - plane) % n_rep, (index + half * (1 - core) + n_z - plane) % n_rep]
-    keep, send = block_rows(jnp.stack([plane, *here]).astype(jnp.int32), slabs, order)
+    keep, send = block_rows(jnp.stack([plane, *here]).astype(jnp.int32), *slabs)
 
     got = lax.ppermute(send, "c", [(0, 1), (1, 0)])
     both = jnp.stack([jnp.where(core == 0, keep, got), jnp.where(core == 0, got, keep)], axis=1)

time: 115 us -> 126 us (1.096)
  starting transfers between devices: 65.9 us -> 70.9 us
  waiting for transfers between devices: 38.4 us -> 42.6 us
  local copies, waits for them, and re-layouts: 2.93 us -> 4.87 us
    all_to_all x1 -> x2, starting transfers between devices: 8.2 us -> 13.2 us  [local(): slabs.append(lax.all_to_all(copies, REP, 0, 0, tiled=True))]
    all_to_all x1 -> x2, waiting for transfers between devices: 14.8 us -> 18.9 us  [local(): slabs.append(lax.all_to_all(copies, REP, 0, 0, tiled=True))]
    unnamed x12, local copies, waits for them, and re-layouts: 0.03 us -> 1.32 us
  transfers between devices with their start and end apart: 6 -> 7, of which waited for: 5 -> 6; matrix products, arithmetic and copies ran while one was open for 1% -> 1% of each run, Pallas kernels for 0% -> 0%
where the time goes in v1:
time: 126 us; the launch traced here: 125 us
  starting transfers between devices  70.9 us (56%)
  waiting for transfers between devices  42.6 us (34%)
  local copies, waits for them, and re-layouts  4.87 us (4%)
  between operations  3.51 us (3%)
  Pallas kernels  2.54 us (2%)
    ppermute x1, starting transfers between devices, local(): slab = lax.ppermute(slab, EVERY, along)  19.6 us
    all_to_all x2, waiting for transfers between devices, local(): slabs.append(lax.all_to_all(copies, REP, 0, 0, tiled=True))  18.9 us
    ppermute x1, starting transfers between devices, local(): both = lax.ppermute(both, EVERY, home)  17.9 us
    all_to_all x1, starting transfers between devices, local(): lax.all_to_all(pieces, EVERY, 0, 0, axis_index_groups=planes, tiled=True)  17.5 us
    all_to_all x2, starting transfers between devices, local(): slabs.append(lax.all_to_all(copies, REP, 0, 0, tiled=True))  13.2 us
    all_to_all x1, waiting for transfers between devices, local(): lax.all_to_all(pieces, EVERY, 0, 0, axis_index_groups=planes, tiled=True)  10.4 us
    ppermute x1, waiting for transfers between devices, local(): both = lax.ppermute(both, EVERY, home)  8.11 us
    ppermute x1, waiting for transfers between devices, local(): slab = lax.ppermute(slab, EVERY, along)  4.16 us
  transfers between devices with their start and end apart: 7, of which 6 were waited for; matrix products, arithmetic and copies ran while one was open for 1% of the time, Pallas kernels for 0%

profile of v1, /device:TPU:8, one launch (start us, length us, event | category | flops | bytes accessed | tf_op | source)
XLA Modules:
  0.0 125.5 jit_solution(836055041383426860)
XLA Ops:
  0.6 0.0 copy-start.1
  0.6 17.5 %all-to-all-start = ((bf16[32,2,16,512]{3,2,1,0:T(8,128)(2,1)}), bf16[32,2,16,512]{3,2,1,0:T(8,128)(2,1)S(1)}, u32[]{:S(2)}, u32[]{:S(2)}) async-start(bf16[32,2,16,512]{3,2,1,0:T(8,128)(2,1)} %bitcast.38), calls=%async_computation | async-start | bytes 2097152 | tf_op jit(solution)/shard_map/all_to_all | solution.py:130
  18.2 0.0 copy-start
  18.2 0.0 copy-start.4
  18.2 0.6 copy-done.4
  18.8 0.6 fusion.6
  20.7 0.0 copy-done.1
  20.7 0.0 copy-done
  20.9 0.7 collective-permute-start
  21.5 10.4 %all-to-all-done = bf16[32,2,16,512]{3,2,1,0:T(8,128)(2,1)S(1)} async-done(((bf16[32,2,16,512]{3,2,1,0:T(8,128)(2,1)}), bf16[32,2,16,512]{3,2,1,0:T(8,128)(2,1)S(1)}, u32[]{:S(2)}, u32[]{:S(2)}) %all-to-all-start) | async-done | bytes 1048608 | tf_op jit(solution)/shard_map/all_to_all | solution.py:130
  32.0 0.2 reduce_sum.12
  32.1 0.0 collective-permute-done
  32.2 19.6 %collective-permute-start.1 = (bf16[2,16,1152]{2,1,0:T(8,128)(2,1)S(1)}, bf16[2,16,1152]{2,1,0:T(8,128)(2,1)S(1)}, u32[]{:S(2)}, u32[]{:S(2)}) collective-permute-start(bf16[2,16,1152]{2,1,0:T(8,128)(2,1)S(1)} %pad_maximum_fusion.1), channel_id=1, source_target_pairs={{512,528},{65,80},{130,144},{195,208},{260,272},{325,336},{390,400... | collective-permute-start | bytes 221192 | tf_op jit(solution)/shard_map/ppermute | solution.py:138
  51.8 4.2 %collective-permute-done.1 = bf16[2,16,1152]{2,1,0:T(8,128)(2,1)S(1)} collective-permute-done((bf16[2,16,1152]{2,1,0:T(8,128)(2,1)S(1)}, bf16[2,16,1152]{2,1,0:T(8,128)(2,1)S(1)}, u32[]{:S(2)}, u32[]{:S(2)}) %collective-permute-start.1) | collective-permute-done | bytes 73760 | tf_op jit(solution)/shard_map/ppermute | solution.py:138
  56.0 0.9 broadcast_in_dim.4
  56.8 8.1 %all-to-all-start.1 = ((bf16[32,16,512]{2,1,0:T(8,128)(2,1)}), bf16[32,16,512]{2,1,0:T(8,128)(2,1)S(1)}, u32[]{:S(2)}, u32[]{:S(2)}) async-start(bf16[32,16,512]{2,1,0:T(8,128)(2,1)} %bitcast.11), calls=%async_computation.1 | async-start | bytes 1048576 | tf_op jit(solution)/shard_map/all_to_all | solution.py:143
  64.9 10.1 %all-to-all-done.1.grads_ref = bf16[32,16,512]{2,1,0:T(8,128)(2,1)S(1)} async-done(((bf16[32,16,512]{2,1,0:T(8,128)(2,1)}), bf16[32,16,512]{2,1,0:T(8,128)(2,1)S(1)}, u32[]{:S(2)}, u32[]{:S(2)}) %all-to-all-start.1) | async-done | bytes 524320 | tf_op jit(solution)/shard_map/all_to_all | solution.py:143
  75.0 0.9 broadcast_in_dim.5
  75.9 5.1 %all-to-all-start.2 = ((bf16[32,16,640]{2,1,0:T(8,128)(2,1)}), bf16[32,16,640]{2,1,0:T(8,128)(2,1)S(1)}, u32[]{:S(2)}, u32[]{:S(2)}) async-start(bf16[32,16,640]{2,1,0:T(8,128)(2,1)} %bitcast.12), calls=%async_computation.2 | async-start | bytes 1310720 | tf_op jit(solution)/shard_map/all_to_all | solution.py:143
  81.0 0.0 copy-start.5
  81.1 0.6 copy-done.5
  81.7 0.6 dynamic_slice.3
  83.6 0.1 pad_add_fusion.where_ref
  83.7 8.8 %all-to-all-done.2.halves_ref = bf16[32,16,640]{2,1,0:T(8,128)(2,1)S(1)} async-done(((bf16[32,16,640]{2,1,0:T(8,128)(2,1)}), bf16[32,16,640]{2,1,0:T(8,128)(2,1)S(1)}, u32[]{:S(2)}, u32[]{:S(2)}) %all-to-all-start.2) | async-done | bytes 655392 | tf_op jit(solution)/shard_map/all_to_all | solution.py:143
  92.5 2.5 %block_rows.1 = (bf16[3,16,512]{2,1,0:T(8,128)(2,1)S(1)}, bf16[3,16,512]{2,1,0:T(8,128)(2,1)S(1)}) custom-call(s32[3]{0:T(128)S(1)} %pad_add_fusion.where_ref, bf16[32,16,512]{2,1,0:T(8,128)(2,1)S(1)} %all-to-all-done.1.grads_ref, bf16[32,16,640]{2,1,0:T(8,128)(2,1)S(1)} %all-to-all-done.2.halves_ref), custom_call_target="tpu_custom_call" | custom-call | tf_op jit(solution)/shard_map/block_rows/pallas_call | solution.py:105
  95.0 2.1 %collective-permute-start.2 = (bf16[3,16,512]{2,1,0:T(8,128)(2,1)S(1)}, bf16[3,16,512]{2,1,0:T(8,128)(2,1)S(1)}, u32[]{:S(2)}, u32[]{:S(2)}) collective-permute-start(bf16[3,16,512]{2,1,0:T(8,128)(2,1)S(1)} %get-tuple-element.6), channel_id=1, source_target_pairs={{0,32},{32,0},{1,33},{33,1},{2,34},{34,2},{3,35},{35,3},{4,36},{36... | collective-permute-start | bytes 147464 | tf_op jit(solution)/shard_map/ppermute | solution.py:148
  97.1 1.0 collective-permute-done.2
  98.2 0.0 copy-start.2
  98.2 0.0 copy-start.3
  98.2 17.9 %collective-permute-start.3 = (bf16[3,2,16,512]{3,2,0,1:T(8,128)(2,1)S(1)}, bf16[3,2,16,512]{3,2,0,1:T(8,128)(2,1)S(1)}, u32[]{:S(2)}, u32[]{:S(2)}) collective-permute-start(bf16[3,2,16,512]{3,2,0,1:T(8,128)(2,1)S(1)} %pad_maximum_fusion), channel_id=1, source_target_pairs={{528,0},{80,1},{144,2},{208,3},{272,4},{336,5},{400,6},{464,7},{16... | collective-permute-start | bytes 294920 | tf_op jit(solution)/shard_map/ppermute | solution.py:150
  116.1 8.1 %collective-permute-done.3 = bf16[3,2,16,512]{3,2,0,1:T(8,128)(2,1)S(1)} collective-permute-done((bf16[3,2,16,512]{3,2,0,1:T(8,128)(2,1)S(1)}, bf16[3,2,16,512]{3,2,0,1:T(8,128)(2,1)S(1)}, u32[]{:S(2)}, u32[]{:S(2)}) %collective-permute-start.3) | collective-permute-done | bytes 98336 | tf_op jit(solution)/shard_map/ppermute | solution.py:150
  124.2 0.6 slice_bitcast_fusion.1
  124.8 0.0 copy-done.2
  124.8 0.0 copy-done.3
  124.8 0.7 fusion
  (11 shorter events, 0.1 us)
Async XLA Ops:
  0.6 20.1 %copy-start.1 = (bf16[2,16,512]{2,1,0:T(8,128)(2,1)S(1)}, bf16[2,16,512]{2,1,0:T(8,128)(2,1)}, u32[]{:S(2)}) copy-start(bf16[2,16,512]{2,1,0:T(8,128)(2,1)} %param.11) | copy-start | bytes 98308
  0.6 31.3 %all-to-all-start = ((bf16[32,2,16,512]{3,2,1,0:T(8,128)(2,1)}), bf16[32,2,16,512]{3,2,1,0:T(8,128)(2,1)S(1)}, u32[]{:S(2)}, u32[]{:S(2)}) async-start(bf16[32,2,16,512]{3,2,1,0:T(8,128)(2,1)} %bitcast.38), calls=%async_computation | async-start | bytes 2097152 | tf_op jit(solution)/shard_map/all_to_all | solution.py:130
  18.2 2.6 %copy-start = (bf16[2,16,512]{2,1,0:T(8,128)(2,1)S(1)}, bf16[2,16,512]{2,1,0:T(8,128)(2,1)}, u32[]{:S(2)}) copy-start(bf16[2,16,512]{2,1,0:T(8,128)(2,1)} %param.12) | copy-start | bytes 98308
  18.2 0.7 copy-start.4
  20.9 11.3 %collective-permute-start = (bf16[2,16,640]{2,1,0:T(8,128)(2,1)S(1)}, bf16[2,16,640]{2,1,0:T(8,128)(2,1)S(1)}, u32[]{:S(2)}, u32[]{:S(2)}) collective-permute-start(bf16[2,16,640]{2,1,0:T(8,128)(2,1)S(1)} %pad_maximum_fusion.3), channel_id=1, source_target_pairs={{0,512},{1,65},{2,130},{3,195},{4,260},{5,325},{6,390},{7,455},{8,... | collective-permute-start | bytes 122888 | tf_op jit(solution)/shard_map/ppermute | solution.py:136
  32.2 23.8 %collective-permute-start.1 = (bf16[2,16,1152]{2,1,0:T(8,128)(2,1)S(1)}, bf16[2,16,1152]{2,1,0:T(8,128)(2,1)S(1)}, u32[]{:S(2)}, u32[]{:S(2)}) collective-permute-start(bf16[2,16,1152]{2,1,0:T(8,128)(2,1)S(1)} %pad_maximum_fusion.1), channel_id=1, source_target_pairs={{512,528},{65,80},{130,144},{195,208},{260,272},{325,336},{390,400... | collective-permute-start | bytes 221192 | tf_op jit(solution)/shard_map/ppermute | solution.py:138
  56.8 18.2 %all-to-all-start.1 = ((bf16[32,16,512]{2,1,0:T(8,128)(2,1)}), bf16[32,16,512]{2,1,0:T(8,128)(2,1)S(1)}, u32[]{:S(2)}, u32[]{:S(2)}) async-start(bf16[32,16,512]{2,1,0:T(8,128)(2,1)} %bitcast.11), calls=%async_computation.1 | async-start | bytes 1048576 | tf_op jit(solution)/shard_map/all_to_all | solution.py:143
  75.9 16.5 %all-to-all-start.2 = ((bf16[32,16,640]{2,1,0:T(8,128)(2,1)}), bf16[32,16,640]{2,1,0:T(8,128)(2,1)S(1)}, u32[]{:S(2)}, u32[]{:S(2)}) async-start(bf16[32,16,640]{2,1,0:T(8,128)(2,1)} %bitcast.12), calls=%async_computation.2 | async-start | bytes 1310720 | tf_op jit(solution)/shard_map/all_to_all | solution.py:143
  81.0 0.7 copy-start.5
  95.0 3.1 %collective-permute-start.2 = (bf16[3,16,512]{2,1,0:T(8,128)(2,1)S(1)}, bf16[3,16,512]{2,1,0:T(8,128)(2,1)S(1)}, u32[]{:S(2)}, u32[]{:S(2)}) collective-permute-start(bf16[3,16,512]{2,1,0:T(8,128)(2,1)S(1)} %get-tuple-element.6), channel_id=1, source_target_pairs={{0,32},{32,0},{1,33},{33,1},{2,34},{34,2},{3,35},{35,3},{4,36},{36... | collective-permute-start | bytes 147464 | tf_op jit(solution)/shard_map/ppermute | solution.py:148
  98.2 26.6 %copy-start.2 = (bf16[2,16,512]{2,1,0:T(8,128)(2,1)S(1)}, bf16[2,16,512]{2,1,0:T(8,128)(2,1)}, u32[]{:S(2)}) copy-start(bf16[2,16,512]{2,1,0:T(8,128)(2,1)} %param.10) | copy-start | bytes 98308
  98.2 26.6 %copy-start.3 = (bf16[2,16,512]{2,1,0:T(8,128)(2,1)S(1)}, bf16[2,16,512]{2,1,0:T(8,128)(2,1)}, u32[]{:S(2)}) copy-start(bf16[2,16,512]{2,1,0:T(8,128)(2,1)} %param.9) | copy-start | bytes 98308
  98.2 26.0 %collective-permute-start.3 = (bf16[3,2,16,512]{3,2,0,1:T(8,128)(2,1)S(1)}, bf16[3,2,16,512]{3,2,0,1:T(8,128)(2,1)S(1)}, u32[]{:S(2)}, u32[]{:S(2)}) collective-permute-start(bf16[3,2,16,512]{3,2,0,1:T(8,128)(2,1)S(1)} %pad_maximum_fusion), channel_id=1, source_target_pairs={{528,0},{80,1},{144,2},{208,3},{272,4},{336,5},{400,6},{464,7},{16... | collective-permute-start | bytes 294920 | tf_op jit(solution)/shard_map/ppermute | solution.py:150

commit v2 on v0

--- a/solution.py
+++ b/solution.py
@@ -139,7 +139,7 @@
 
     slabs = jnp.broadcast_to(slab[None], (half, *slab.shape)).reshape(n_rep, n_rows, slab.shape[-1])
     slabs = lax.all_to_all(slabs, REP, 0, 0, tiled=True)
-    index = jnp.array([index_of(2 * xy, half) for xy in range(half)], jnp.int32)[my_xy]
+    index = half + jnp.where(my_xy == 0, half // 2, jnp.where(my_xy == half // 2, 0, my_xy))
     here = [(index + half * core + n_z - plane) % n_rep, (index + half * (1 - core) + n_z - plane) % n_rep]
     keep, send = block_rows(jnp.stack([plane, *here]).astype(jnp.int32), slabs, order)
 

time: 115 us -> 115 us (level)
  waiting for transfers between devices: 38.4 us -> 40.3 us
  between operations: 3.51 us -> 2.2 us
    all_to_all x1, waiting for transfers between devices: 14.8 us -> 16.7 us  [local(): slabs = lax.all_to_all(slabs, REP, 0, 0, tiled=True)]
where the time goes in v2:
time: 115 us; the launch traced here: 114 us
  starting transfers between devices  65.7 us (57%)
  waiting for transfers between devices  40.3 us (35%)
  Pallas kernels  2.55 us (2%)
  local copies, waits for them, and re-layouts  2.35 us (2%)
  between operations  2.2 us (2%)
    ppermute x1, starting transfers between devices, local(): slab = lax.ppermute(slab, EVERY, along)  19.6 us
    ppermute x1, starting transfers between devices, local(): both = lax.ppermute(both, EVERY, home)  17.8 us
    all_to_all x1, starting transfers between devices, local(): lax.all_to_all(pieces, EVERY, 0, 0, axis_index_groups=planes, tiled=True)  17.6 us
    all_to_all x1, waiting for transfers between devices, local(): slabs = lax.all_to_all(slabs, REP, 0, 0, tiled=True)  16.7 us
    all_to_all x1, waiting for transfers between devices, local(): lax.all_to_all(pieces, EVERY, 0, 0, axis_index_groups=planes, tiled=True)  11.1 us
    all_to_all x1, starting transfers between devices, local(): slabs = lax.all_to_all(slabs, REP, 0, 0, tiled=True)  8.07 us
    ppermute x1, waiting for transfers between devices, local(): both = lax.ppermute(both, EVERY, home)  7.08 us
    ppermute x1, waiting for transfers between devices, local(): slab = lax.ppermute(slab, EVERY, along)  4.16 us
  transfers between devices with their start and end apart: 6, of which 5 were waited for; matrix products, arithmetic and copies ran while one was open for 1% of the time, Pallas kernels for 0%

profile of v2, /device:TPU:8, one launch (start us, length us, event | category | flops | bytes accessed | tf_op | source)
XLA Modules:
  0.0 114.1 jit_solution(14315034470112961543)
XLA Ops:
  0.6 0.0 copy-start.4
  0.6 0.0 copy-start
  0.7 0.0 copy-start.1
  0.7 17.6 %all-to-all-start = ((bf16[32,2,16,512]{3,2,1,0:T(8,128)(2,1)}), bf16[32,2,16,512]{3,2,1,0:T(8,128)(2,1)S(1)}, u32[]{:S(2)}, u32[]{:S(2)}) async-start(bf16[32,2,16,512]{3,2,1,0:T(8,128)(2,1)} %bitcast.36), calls=%async_computation | async-start | bytes 2097152 | tf_op jit(solution)/shard_map/all_to_all | solution.py:130
  18.3 0.0 copy-done.4
  18.3 0.6 fusion.6
  20.2 0.0 copy-done
  20.2 0.0 copy-done.1
  20.4 0.7 collective-permute-start
  21.0 11.1 %all-to-all-done = bf16[32,2,16,512]{3,2,1,0:T(8,128)(2,1)S(1)} async-done(((bf16[32,2,16,512]{3,2,1,0:T(8,128)(2,1)}), bf16[32,2,16,512]{3,2,1,0:T(8,128)(2,1)S(1)}, u32[]{:S(2)}, u32[]{:S(2)}) %all-to-all-start) | async-done | bytes 1048608 | tf_op jit(solution)/shard_map/all_to_all | solution.py:130
  32.1 0.2 reduce_sum.12
  32.3 0.0 collective-permute-done
  32.3 19.6 %collective-permute-start.1 = (bf16[2,16,1152]{2,1,0:T(8,128)(2,1)S(1)}, bf16[2,16,1152]{2,1,0:T(8,128)(2,1)S(1)}, u32[]{:S(2)}, u32[]{:S(2)}) collective-permute-start(bf16[2,16,1152]{2,1,0:T(8,128)(2,1)S(1)} %pad_maximum_fusion.1), channel_id=1, source_target_pairs={{512,528},{65,80},{130,144},{195,208},{260,272},{325,336},{390,400... | collective-permute-start | bytes 221192 | tf_op jit(solution)/shard_map/ppermute | solution.py:138
  51.9 4.2 %collective-permute-done.1 = bf16[2,16,1152]{2,1,0:T(8,128)(2,1)S(1)} collective-permute-done((bf16[2,16,1152]{2,1,0:T(8,128)(2,1)S(1)}, bf16[2,16,1152]{2,1,0:T(8,128)(2,1)S(1)}, u32[]{:S(2)}, u32[]{:S(2)}) %collective-permute-start.1) | collective-permute-done | bytes 73760 | tf_op jit(solution)/shard_map/ppermute | solution.py:138
  56.1 1.1 broadcast_in_dim.2
  57.2 8.1 %all-to-all-start.1 = ((bf16[32,16,1152]{2,1,0:T(8,128)(2,1)}), bf16[32,16,1152]{2,1,0:T(8,128)(2,1)S(1)}, u32[]{:S(2)}, u32[]{:S(2)}) async-start(bf16[32,16,1152]{2,1,0:T(8,128)(2,1)} %bitcast.10), calls=%async_computation.1 | async-start | bytes 2359296 | tf_op jit(solution)/shard_map/all_to_all | solution.py:141
  65.3 0.0 copy-start.2
  65.3 0.0 copy-start.3
  65.4 0.1 pad_add_fusion.where_ref
  65.4 16.7 %all-to-all-done.1.slabs_ref = bf16[32,16,1152]{2,1,0:T(8,128)(2,1)S(1)} async-done(((bf16[32,16,1152]{2,1,0:T(8,128)(2,1)}), bf16[32,16,1152]{2,1,0:T(8,128)(2,1)S(1)}, u32[]{:S(2)}, u32[]{:S(2)}) %all-to-all-start.1) | async-done | bytes 1179680 | tf_op jit(solution)/shard_map/all_to_all | solution.py:141
  82.2 2.6 %block_rows.1 = (bf16[3,16,512]{2,1,0:T(8,128)(2,1)S(1)}, bf16[3,16,512]{2,1,0:T(8,128)(2,1)S(1)}) custom-call(s32[3]{0:T(128)S(1)} %pad_add_fusion.where_ref, bf16[32,16,1152]{2,1,0:T(8,128)(2,1)S(1)} %all-to-all-done.1.slabs_ref), custom_call_target="tpu_custom_call" | custom-call | tf_op jit(solution)/shard_map/block_rows/pallas_call | solution.py:105
  84.7 1.9 %collective-permute-start.2 = (bf16[3,16,512]{2,1,0:T(8,128)(2,1)S(1)}, bf16[3,16,512]{2,1,0:T(8,128)(2,1)S(1)}, u32[]{:S(2)}, u32[]{:S(2)}) collective-permute-start(bf16[3,16,512]{2,1,0:T(8,128)(2,1)S(1)} %get-tuple-element.6), channel_id=1, source_target_pairs={{0,32},{32,0},{1,33},{33,1},{2,34},{34,2},{3,35},{35,3},{4,36},{36... | collective-permute-start | bytes 147464 | tf_op jit(solution)/shard_map/ppermute | solution.py:146
  86.7 1.2 %collective-permute-done.2 = bf16[3,16,512]{2,1,0:T(8,128)(2,1)S(1)} collective-permute-done((bf16[3,16,512]{2,1,0:T(8,128)(2,1)S(1)}, bf16[3,16,512]{2,1,0:T(8,128)(2,1)S(1)}, u32[]{:S(2)}, u32[]{:S(2)}) %collective-permute-start.2) | collective-permute-done | bytes 49184 | tf_op jit(solution)/shard_map/ppermute | solution.py:146
  87.9 17.8 %collective-permute-start.3 = (bf16[3,2,16,512]{3,2,0,1:T(8,128)(2,1)S(1)}, bf16[3,2,16,512]{3,2,0,1:T(8,128)(2,1)S(1)}, u32[]{:S(2)}, u32[]{:S(2)}) collective-permute-start(bf16[3,2,16,512]{3,2,0,1:T(8,128)(2,1)S(1)} %pad_maximum_fusion), channel_id=1, source_target_pairs={{528,0},{80,1},{144,2},{208,3},{272,4},{336,5},{400,6},{464,7},{16... | collective-permute-start | bytes 294920 | tf_op jit(solution)/shard_map/ppermute | solution.py:148
  105.7 7.1 %collective-permute-done.3 = bf16[3,2,16,512]{3,2,0,1:T(8,128)(2,1)S(1)} collective-permute-done((bf16[3,2,16,512]{3,2,0,1:T(8,128)(2,1)S(1)}, bf16[3,2,16,512]{3,2,0,1:T(8,128)(2,1)S(1)}, u32[]{:S(2)}, u32[]{:S(2)}) %collective-permute-start.3) | collective-permute-done | bytes 98336 | tf_op jit(solution)/shard_map/ppermute | solution.py:148
  112.8 0.6 slice_bitcast_fusion.1
  113.4 0.0 copy-done.2
  113.4 0.0 copy-done.3
  113.4 0.7 fusion
  (9 shorter events, 0.1 us)
Async XLA Ops:
  0.6 17.7 %copy-start.4 = (s32[2]{0:T(128)S(1)}, s32[2]{0:T(128)}, u32[]{:S(2)}) copy-start(s32[2]{0:T(128)} %param.7) | copy-start | bytes 28
  0.6 19.6 %copy-start = (bf16[2,16,512]{2,1,0:T(8,128)(2,1)S(1)}, bf16[2,16,512]{2,1,0:T(8,128)(2,1)}, u32[]{:S(2)}) copy-start(bf16[2,16,512]{2,1,0:T(8,128)(2,1)} %param.11) | copy-start | bytes 98308
  0.7 19.6 %copy-start.1 = (bf16[2,16,512]{2,1,0:T(8,128)(2,1)S(1)}, bf16[2,16,512]{2,1,0:T(8,128)(2,1)}, u32[]{:S(2)}) copy-start(bf16[2,16,512]{2,1,0:T(8,128)(2,1)} %param.10) | copy-start | bytes 98308
  0.7 31.5 %all-to-all-start = ((bf16[32,2,16,512]{3,2,1,0:T(8,128)(2,1)}), bf16[32,2,16,512]{3,2,1,0:T(8,128)(2,1)S(1)}, u32[]{:S(2)}, u32[]{:S(2)}) async-start(bf16[32,2,16,512]{3,2,1,0:T(8,128)(2,1)} %bitcast.36), calls=%async_computation | async-start | bytes 2097152 | tf_op jit(solution)/shard_map/all_to_all | solution.py:130
  20.4 11.9 %collective-permute-start = (bf16[2,16,640]{2,1,0:T(8,128)(2,1)S(1)}, bf16[2,16,640]{2,1,0:T(8,128)(2,1)S(1)}, u32[]{:S(2)}, u32[]{:S(2)}) collective-permute-start(bf16[2,16,640]{2,1,0:T(8,128)(2,1)S(1)} %pad_maximum_fusion.3), channel_id=1, source_target_pairs={{0,512},{1,65},{2,130},{3,195},{4,260},{5,325},{6,390},{7,455},{8,... | collective-permute-start | bytes 122888 | tf_op jit(solution)/shard_map/ppermute | solution.py:136
  32.3 23.8 %collective-permute-start.1 = (bf16[2,16,1152]{2,1,0:T(8,128)(2,1)S(1)}, bf16[2,16,1152]{2,1,0:T(8,128)(2,1)S(1)}, u32[]{:S(2)}, u32[]{:S(2)}) collective-permute-start(bf16[2,16,1152]{2,1,0:T(8,128)(2,1)S(1)} %pad_maximum_fusion.1), channel_id=1, source_target_pairs={{512,528},{65,80},{130,144},{195,208},{260,272},{325,336},{390,400... | collective-permute-start | bytes 221192 | tf_op jit(solution)/shard_map/ppermute | solution.py:138
  57.2 24.9 %all-to-all-start.1 = ((bf16[32,16,1152]{2,1,0:T(8,128)(2,1)}), bf16[32,16,1152]{2,1,0:T(8,128)(2,1)S(1)}, u32[]{:S(2)}, u32[]{:S(2)}) async-start(bf16[32,16,1152]{2,1,0:T(8,128)(2,1)} %bitcast.10), calls=%async_computation.1 | async-start | bytes 2359296 | tf_op jit(solution)/shard_map/all_to_all | solution.py:141
  65.3 48.1 %copy-start.2 = (bf16[2,16,512]{2,1,0:T(8,128)(2,1)S(1)}, bf16[2,16,512]{2,1,0:T(8,128)(2,1)}, u32[]{:S(2)}) copy-start(bf16[2,16,512]{2,1,0:T(8,128)(2,1)} %param.9) | copy-start | bytes 98308
  65.3 48.1 %copy-start.3 = (bf16[2,16,512]{2,1,0:T(8,128)(2,1)S(1)}, bf16[2,16,512]{2,1,0:T(8,128)(2,1)}, u32[]{:S(2)}) copy-start(bf16[2,16,512]{2,1,0:T(8,128)(2,1)} %param.8) | copy-start | bytes 98308
  84.7 3.1 %collective-permute-start.2 = (bf16[3,16,512]{2,1,0:T(8,128)(2,1)S(1)}, bf16[3,16,512]{2,1,0:T(8,128)(2,1)S(1)}, u32[]{:S(2)}, u32[]{:S(2)}) collective-permute-start(bf16[3,16,512]{2,1,0:T(8,128)(2,1)S(1)} %get-tuple-element.6), channel_id=1, source_target_pairs={{0,32},{32,0},{1,33},{33,1},{2,34},{34,2},{3,35},{35,3},{4,36},{36... | collective-permute-start | bytes 147464 | tf_op jit(solution)/shard_map/ppermute | solution.py:146
  87.9 24.9 %collective-permute-start.3 = (bf16[3,2,16,512]{3,2,0,1:T(8,128)(2,1)S(1)}, bf16[3,2,16,512]{3,2,0,1:T(8,128)(2,1)S(1)}, u32[]{:S(2)}, u32[]{:S(2)}) collective-permute-start(bf16[3,2,16,512]{3,2,0,1:T(8,128)(2,1)S(1)} %pad_maximum_fusion), channel_id=1, source_target_pairs={{528,0},{80,1},{144,2},{208,3},{272,4},{336,5},{400,6},{464,7},{16... | collective-permute-start | bytes 294920 | tf_op jit(solution)/shard_map/ppermute | solution.py:148
